TPU v7x, 32 devices: a whole 2x2x4 slice. The times are simulated.
32 devices in a mesh: dp: 8 (over y, x, core), tensor: 4 (over z).
Axes of the slice: x: 2, y: 2, z: 4, core: 2. Of those that a mesh axis runs over, the one named last changes fastest.
Arguments:
- tokens: bfloat16 [1024, 8192], P('dp', 'tensor'), may hold values from -6 to 6
- cotangent: bfloat16 [1024, 8192], P('dp', 'tensor'), may hold values from -6 to 6
- up_blocks: bfloat16 [3, 64, 128, 256], P(None, 'tensor'), may hold values from -0.21875 to 0.21875
- up_left: bfloat16 [8192, 128], P('tensor'), may hold values from -0.0625 to 0.0625
- up_right: bfloat16 [128, 16384], P(None, 'tensor'), may hold values from -0.375 to 0.375
- down_blocks: bfloat16 [3, 64, 256, 128], P(None, 'tensor'), may hold values from -0.15625 to 0.15625
- down_left: bfloat16 [16384, 128], P('tensor'), may hold values from -0.046875 to 0.046875
- down_right: bfloat16 [128, 8192], P(None, 'tensor'), may hold values from -0.375 to 0.375
Outputs:
- out: bfloat16 [1024, 8192], P('dp', 'tensor')
- tokens_grad: bfloat16 [1024, 8192], P('dp', 'tensor')
- up_blocks_grad: bfloat16 [3, 64, 128, 256], P(None, 'tensor', 'dp')
- up_left_grad: bfloat16 [8192, 128], P('tensor', 'dp')
- up_right_grad: bfloat16 [128, 16384], P('dp', 'tensor')
- down_blocks_grad: bfloat16 [3, 64, 256, 128], P(None, 'tensor', 'dp')
- down_left_grad: bfloat16 [16384, 128], P('tensor', 'dp')
- down_right_grad: bfloat16 [128, 8192], P('dp', 'tensor')
All inputs are finite; a program needn't handle non-finite values.
Results may differ from a plain program's by a relative error of at most 0.03.
Values may be sent and summed in bfloat16 or wider, within the bound.
A program may use at most 64 MiB of HBM per device.

v0:
```python
import math

import jax
import jax.numpy as jnp
from jax import lax
from jax.sharding import PartitionSpec as P


def partner(block, axis, bit):
    count = lax.axis_size(axis)
    route = []
    for low in range(count):
        high = low | 1 << bit
        if high != low and high < count:
            route += [(low, high), (high, low)]
    return lax.ppermute(block, axis, route)


def smooth_gate(values):
    return jax.nn.gelu(values, approximate=False)


def blockwise(left, blocks, form, width_out):
    row_count = left.shape[0]
    block_count = blocks.shape[0]
    pieces = left.reshape(row_count, block_count, -1)
    result = jnp.einsum(form, pieces, blocks, preferred_element_type=jnp.float32)
    return result.reshape(row_count, block_count * width_out)


def block_outer(left, right, block_count, form):
    row_count = left.shape[0]
    left_pieces = left.reshape(row_count, block_count, -1)
    right_pieces = right.reshape(row_count, block_count, -1)
    return jnp.einsum(form, left_pieces, right_pieces, preferred_element_type=jnp.float32)


def body(tokens, cotangent, up_blocks, up_left, up_right, down_blocks, down_left, down_right):
    row_count = tokens.shape[0]
    block_count = up_blocks.shape[1]
    block_side = up_blocks.shape[2]
    hidden_side = up_blocks.shape[3]
    sections = lax.axis_size("tensor").bit_length() - 1
    section_bits = list(range(sections))
    grad_scale = 1.0 / math.sqrt(row_count * lax.axis_size("dp"))
    low_sums = lax.psum(
        (
            jnp.dot(tokens, up_left, preferred_element_type=jnp.float32),
            jnp.einsum("nd,rd->nr", cotangent, down_right, preferred_element_type=jnp.float32),
        ),
        "tensor",
    )
    low_up = low_sums[0].astype(jnp.bfloat16)
    low_cot = low_sums[1].astype(jnp.bfloat16)
    hidden_pre = blockwise(tokens, up_blocks[0], "nbi,bih->nbh", hidden_side)
    hidden_pre = hidden_pre + jnp.dot(low_up, up_right, preferred_element_type=jnp.float32)
    partner_tokens = {}
    partner_cot = {}
    for section_bit in section_bits:
        arrived = partner((tokens, cotangent), "tensor", section_bit)
        partner_tokens[section_bit] = arrived[0]
        partner_cot[section_bit] = arrived[1]
        hidden_pre = hidden_pre + blockwise(
            arrived[0], up_blocks[section_bit + 1], "nbi,bih->nbh", hidden_side
        )
    active, gelu_back = jax.vjp(smooth_gate, hidden_pre)
    hidden = active.astype(jnp.bfloat16)
    low_down = lax.psum(
        jnp.dot(hidden, down_left, preferred_element_type=jnp.float32), "tensor"
    ).astype(jnp.bfloat16)
    out_sum = blockwise(hidden, down_blocks[0], "nbh,bhi->nbi", block_side)
    out_sum = out_sum + jnp.dot(low_down, down_right, preferred_element_type=jnp.float32)
    for section_bit in section_bits:
        partial_out = blockwise(hidden, down_blocks[section_bit + 1], "nbh,bhi->nbi", block_side)
        out_sum = out_sum + partner(partial_out, "tensor", section_bit)
    out = out_sum.astype(jnp.bfloat16)
    hidden_grad = jnp.einsum("nr,hr->nh", low_cot, down_left, preferred_element_type=jnp.float32)
    hidden_grad = hidden_grad + blockwise(cotangent, down_blocks[0], "nbi,bhi->nbh", hidden_side)
    for section_bit in section_bits:
        hidden_grad = hidden_grad + blockwise(
            partner_cot[section_bit], down_blocks[section_bit + 1], "nbi,bhi->nbh", hidden_side
        )
    down_block_terms = (
        jnp.stack(
            [block_outer(hidden, cotangent, block_count, "nbh,nbi->bhi")]
            + [
                block_outer(hidden, partner_cot[section], block_count, "nbh,nbi->bhi")
                for section in range(sections)
            ]
        )
        * grad_scale
    )
    down_left_terms = (
        jnp.einsum("nh,nr->hr", hidden, low_cot, preferred_element_type=jnp.float32) * grad_scale
    )
    down_right_terms = (
        jnp.einsum("nr,nd->rd", low_down, cotangent, preferred_element_type=jnp.float32)
        * grad_scale
    )
    pre_grad = gelu_back(hidden_grad)[0].astype(jnp.bfloat16)
    low_pre = lax.psum(
        jnp.einsum("nh,rh->nr", pre_grad, up_right, preferred_element_type=jnp.float32), "tensor"
    ).astype(jnp.bfloat16)
    tokens_sum = jnp.einsum("nr,dr->nd", low_pre, up_left, preferred_element_type=jnp.float32)
    tokens_sum = tokens_sum + blockwise(pre_grad, up_blocks[0], "nbh,bih->nbi", block_side)
    for section_bit in section_bits:
        partial_grad = blockwise(pre_grad, up_blocks[section_bit + 1], "nbh,bih->nbi", block_side)
        tokens_sum = tokens_sum + partner(partial_grad, "tensor", section_bit)
    tokens_grad = tokens_sum.astype(jnp.bfloat16)
    up_block_terms = (
        jnp.stack(
            [block_outer(tokens, pre_grad, block_count, "nbi,nbh->bih")]
            + [
                block_outer(partner_tokens[section], pre_grad, block_count, "nbi,nbh->bih")
                for section in range(sections)
            ]
        )
        * grad_scale
    )
    up_left_terms = (
        jnp.einsum("nd,nr->dr", tokens, low_pre, preferred_element_type=jnp.float32) * grad_scale
    )
    up_right_terms = (
        jnp.einsum("nr,nh->rh", low_up, pre_grad, preferred_element_type=jnp.float32) * grad_scale
    )
    summed = (
        lax.psum_scatter(
            up_block_terms.astype(jnp.bfloat16), "dp", scatter_dimension=2, tiled=True
        ).astype(jnp.float32),
        lax.psum_scatter(
            up_left_terms.astype(jnp.bfloat16), "dp", scatter_dimension=1, tiled=True
        ).astype(jnp.float32),
        lax.psum_scatter(
            up_right_terms.astype(jnp.bfloat16), "dp", scatter_dimension=0, tiled=True
        ).astype(jnp.float32),
        lax.psum_scatter(
            down_block_terms.astype(jnp.bfloat16), "dp", scatter_dimension=2, tiled=True
        ).astype(jnp.float32),
        lax.psum_scatter(
            down_left_terms.astype(jnp.bfloat16), "dp", scatter_dimension=1, tiled=True
        ).astype(jnp.float32),
        lax.psum_scatter(
            down_right_terms.astype(jnp.bfloat16), "dp", scatter_dimension=0, tiled=True
        ).astype(jnp.float32),
    )
    grads = tuple((total.astype(jnp.bfloat16) for total in summed))
    return (out, tokens_grad, grads[0], grads[1], grads[2], grads[3], grads[4], grads[5])


def solution(mesh):
    in_specs = (
        P("dp", "tensor"),
        P("dp", "tensor"),
        P(None, "tensor", None, None),
        P("tensor", None),
        P(None, "tensor"),
        P(None, "tensor", None, None),
        P("tensor", None),
        P(None, "tensor"),
    )
    out_specs = (
        P("dp", "tensor"),
        P("dp", "tensor"),
        P(None, "tensor", "dp", None),
        P("tensor", "dp"),
        P("dp", "tensor"),
        P(None, "tensor", "dp", None),
        P("tensor", "dp"),
        P("dp", "tensor"),
    )
    return jax.shard_map(body, mesh=mesh, in_specs=in_specs, out_specs=out_specs, check_vma=False)
```

profile of v0, /device:TPU:0, one launch (start us, length us, event | category | flops | bytes accessed | tf_op | source)
XLA Modules:
  0.0 377.2 jit_solution(16703132009617652408)
XLA Ops:
  7.3 2.2 copy.133
  9.5 4.0 %collective-permute-start.5 = (bf16[128,2048]{0,1:T(8,128)(2,1)}, bf16[128,2048]{0,1:T(8,128)(2,1)}, u32[]{:S(2)}, u32[]{:S(2)}) collective-permute-start(bf16[128,2048]{0,1:T(8,128)(2,1)} %copy.133), channel_id=1, source_target_pairs={{0,2},{2,0},{1,3},{3,1},{4,6},{6,4},{5,7},{7,5},{8,10},{10,8},{9,1... | collective-permute-start | bytes 1572872 | tf_op jit(solution)/shard_map/ppermute | solution.py:16
  18.2 3.1 fusion.41
  21.3 3.0 copy.112
  24.3 49.9 %all-reduce.4 = (bf16[128,128]{1,0:T(8,128)(2,1)S(1)}, bf16[128,128]{1,0:T(8,128)(2,1)S(1)}) all-reduce(f32[128,128]{1,0:T(8,128)S(1)} %fusion.72, f32[128,128]{1,0:T(8,128)S(1)} %fusion.74), channel_id=1, replica_groups=mesh['dp'=8,'tensor'=4] {'tensor'}, use_global_device_ids=true, to_apply=%region_0.0 | all-reduce | flops 32768 | bytes 196608 | tf_op jit(solution)/shard_map/psum | solution.py:46
  74.3 3.4 convolution_add_fusion.1
  77.7 3.0 fusion.27
  99.0 9.3 %add_convert_fusion = (bf16[128,4096]{1,0:T(8,128)(2,1)S(1)}, f32[128,4096]{1,0:T(8,128)}, f32[128,4096]{1,0:T(8,128)}) fusion(f32[128,4096]{1,0:T(8,128)} %copy.184, f32[128,4096]{1,0:T(8,128)} %convolution_add_fusion, f32[128,4096]{1,0:T(8,128)} %copy.183, f32[128,4096]{1,0:T(8,128)} %copy.179, f32[128,4096]{1,0:T(8,128)} %convolution_add_fusion.1, ...), kind=kLoop, calls=%fused_computation.25 | loop fusion | flops 39845888 | bytes 17825792 | tf_op jit(solution)/shard_map/convert_element_type | solution.py:100
  114.4 4.9 %copy.156 = bf16[3,16,128,256]{3,1,0,2:T(8,128)(2,1)} copy(bf16[3,16,128,256]{2,3,1,0:T(8,128)(2,1)} %fusion) | data formatting | bytes 6291456 | tf_op jit(solution)/shard_map/convert_element_type | solution.py:128
  119.6 2.5 multiply_convert_fusion
  124.7 18.1 %all-reduce.5 = (bf16[128,128]{1,0:T(8,128)(2,1)S(1)}, bf16[128,128]{1,0:T(8,128)(2,1)S(1)}) all-reduce(f32[128,128]{1,0:T(8,128)S(1)} %fusion.73, f32[128,128]{1,0:T(8,128)S(1)} %fusion.75), channel_id=1, replica_groups=mesh['dp'=8,'tensor'=4] {'tensor'}, use_global_device_ids=true, to_apply=%region_1.0 | all-reduce | flops 32768 | bytes 196608 | tf_op jit(solution)/shard_map/psum | solution.py:68
  145.1 2.2 fusion.12
  147.3 2.7 fusion.3
  158.9 2.7 fusion.21
  161.6 2.6 copy.181
  164.2 2.7 fusion.25
  166.9 2.5 copy.180
  169.4 2.4 collective-permute-start.3
  171.8 2.6 fusion.35
  174.4 2.6 copy.186
  177.0 2.6 fusion.31
  179.6 2.6 copy.187
  184.8 2.7 fusion.39
  187.4 2.6 copy.185
  192.1 18.8 %collective-permute-done.2 = f32[128,2048]{1,0:T(8,128)} collective-permute-done((f32[128,2048]{1,0:T(8,128)}, f32[128,2048]{1,0:T(8,128)}, u32[]{:S(2)}, u32[]{:S(2)}) %collective-permute-start.2) | collective-permute-done | bytes 1048608 | tf_op jit(solution)/shard_map/ppermute | solution.py:16
  210.9 30.8 %collective-permute-done.3 = f32[128,2048]{1,0:T(8,128)} collective-permute-done((f32[128,2048]{1,0:T(8,128)}, f32[128,2048]{1,0:T(8,128)}, u32[]{:S(2)}, u32[]{:S(2)}) %collective-permute-start.3) | collective-permute-done | bytes 1048608 | tf_op jit(solution)/shard_map/ppermute | solution.py:16
  241.7 2.8 fusion.8
  244.4 11.9 %collective-permute-done.7 = f32[128,2048]{1,0:T(8,128)} collective-permute-done((f32[128,2048]{1,0:T(8,128)}, f32[128,2048]{1,0:T(8,128)}, u32[]{:S(2)}, u32[]{:S(2)}) %collective-permute-start.7) | collective-permute-done | bytes 1048608 | tf_op jit(solution)/shard_map/ppermute | solution.py:16
  256.3 2.6 fusion.9
  260.9 19.1 %reduce-scatter.15.cloned.1.call-done = bf16[4096,16]{0,1:T(8,128)(2,1)} async-done(((bf16[4096,128]{0,1:T(8,128)(2,1)}), bf16[4096,16]{0,1:T(8,128)(2,1)}) %reduce-scatter.15.cloned.1.call-update) | async-done | bytes 131088 | tf_op jit(solution)/shard_map/reduce_scatter | solution.py:139
  280.0 40.0 %reduce-scatter.11.cloned.1.call-done = bf16[16,4096]{1,0:T(8,128)(2,1)} async-done(((bf16[128,4096]{1,0:T(8,128)(2,1)}), bf16[16,4096]{1,0:T(8,128)(2,1)}) %reduce-scatter.11.cloned.1.call-update) | async-done | bytes 131088 | tf_op jit(solution)/shard_map/reduce_scatter | solution.py:133
  319.9 50.4 %reduce-scatter.13.cloned.1.call-done = bf16[3,16,32,128]{3,2,1,0:T(8,128)(2,1)} async-done(((bf16[3,16,256,128]{3,2,1,0:T(8,128)(2,1)}), bf16[3,16,32,128]{3,2,1,0:T(8,128)(2,1)}) %reduce-scatter.13.cloned.1.call-update) | async-done | bytes 393232 | tf_op jit(solution)/shard_map/reduce_scatter | solution.py:136
  (80 shorter events, 49.6 us)
Async XLA Ops:
  7.2 75.4 %copy-start = (bf16[4096,128]{1,0:T(8,128)(2,1)S(1)}, bf16[4096,128]{1,0:T(8,128)(2,1)}, u32[]{:S(2)}) copy-start(bf16[4096,128]{1,0:T(8,128)(2,1)} %param.14) | copy-start | bytes 3145732
  7.2 10.7 %copy-start.4 = (bf16[128,2048]{1,0:T(8,128)(2,1)S(1)}, bf16[128,2048]{1,0:T(8,128)(2,1)}, u32[]{:S(2)}) copy-start(bf16[128,2048]{1,0:T(8,128)(2,1)} %param.9) | copy-start | bytes 1572868
  7.2 10.4 %copy-start.2 = (bf16[128,2048]{1,0:T(8,128)(2,1)S(1)}, bf16[128,2048]{1,0:T(8,128)(2,1)}, u32[]{:S(2)}) copy-start(bf16[128,2048]{1,0:T(8,128)(2,1)} %param.8) | copy-start | bytes 1572868
  7.2 10.4 %copy-start.10 = (bf16[2048,128]{1,0:T(8,128)(2,1)S(1)}, bf16[2048,128]{1,0:T(8,128)(2,1)}, u32[]{:S(2)}) copy-start(bf16[2048,128]{1,0:T(8,128)(2,1)} %param.11) | copy-start | bytes 1572868
  7.2 10.7 %copy-start.9 = (bf16[128,2048]{1,0:T(8,128)(2,1)S(1)}, bf16[128,2048]{1,0:T(8,128)(2,1)}, u32[]{:S(2)}) copy-start(bf16[128,2048]{1,0:T(8,128)(2,1)} %param.15) | copy-start | bytes 1572868
  7.2 251.8 %reduce-scatter.7.cloned.1.call-start = ((), (), s32[]{:S(2)}) async-start(), calls=%async_computation.6 | async-start | bytes 3538944 | tf_op jit(solution)/shard_map/reduce_scatter | solution.py:127
  9.5 85.9 %collective-permute-start.5 = (bf16[128,2048]{0,1:T(8,128)(2,1)}, bf16[128,2048]{0,1:T(8,128)(2,1)}, u32[]{:S(2)}, u32[]{:S(2)}) collective-permute-start(bf16[128,2048]{0,1:T(8,128)(2,1)} %copy.133), channel_id=1, source_target_pairs={{0,2},{2,0},{1,3},{3,1},{4,6},{6,4},{5,7},{7,5},{8,10},{10,8},{9,1... | collective-permute-start | bytes 1572872 | tf_op jit(solution)/shard_map/ppermute | solution.py:16
  13.5 78.2 %collective-permute-start.4 = (bf16[128,2048]{0,1:T(8,128)(2,1)}, bf16[128,2048]{0,1:T(8,128)(2,1)}, u32[]{:S(2)}, u32[]{:S(2)}) collective-permute-start(bf16[128,2048]{0,1:T(8,128)(2,1)} %copy.133), channel_id=1, source_target_pairs={{0,1},{1,0},{2,3},{3,2},{4,5},{5,4},{6,7},{7,6},{8,9},{9,8},{10,11... | collective-permute-start | bytes 1572872 | tf_op jit(solution)/shard_map/ppermute | solution.py:16
  17.1 70.9 %collective-permute-start.1 = (bf16[128,2048]{0,1:T(8,128)(2,1)}, bf16[128,2048]{0,1:T(8,128)(2,1)}, u32[]{:S(2)}, u32[]{:S(2)}) collective-permute-start(bf16[128,2048]{0,1:T(8,128)(2,1)} %copy.114), channel_id=1, source_target_pairs={{0,2},{2,0},{1,3},{3,1},{4,6},{6,4},{5,7},{7,5},{8,10},{10,8},{9,1... | collective-permute-start | bytes 1572872 | tf_op jit(solution)/shard_map/ppermute | solution.py:16
  17.5 66.9 %collective-permute-start = (bf16[128,2048]{0,1:T(8,128)(2,1)}, bf16[128,2048]{0,1:T(8,128)(2,1)}, u32[]{:S(2)}, u32[]{:S(2)}) collective-permute-start(bf16[128,2048]{0,1:T(8,128)(2,1)} %copy.114), channel_id=1, source_target_pairs={{0,1},{1,0},{2,3},{3,2},{4,5},{5,4},{6,7},{7,6},{8,9},{9,8},{10,11... | collective-permute-start | bytes 1572872 | tf_op jit(solution)/shard_map/ppermute | solution.py:16
  21.2 53.0 %copy-start.6 = (bf16[128,4096]{1,0:T(8,128)(2,1)S(1)}, bf16[128,4096]{1,0:T(8,128)(2,1)}, u32[]{:S(2)}) copy-start(bf16[128,4096]{1,0:T(8,128)(2,1)} %param.12) | copy-start | bytes 3145732
  110.4 1.5 copy-start.3
  119.3 141.5 %reduce-scatter.17.cloned.1.call-start = ((), (), s32[]{:S(2)}) async-start(), calls=%async_computation.11 | async-start | bytes 589824 | tf_op jit(solution)/shard_map/reduce_scatter | solution.py:142
  122.0 1.0 copy-start.1
  123.0 1.2 copy-start.7
  145.0 115.8 %reduce-scatter.9.cloned.1.call-start = ((), (), s32[]{:S(2)}) async-start(), calls=%async_computation.7 | async-start | bytes 589824 | tf_op jit(solution)/shard_map/reduce_scatter | solution.py:130
  147.3 132.7 %reduce-scatter.15.cloned.1.call-start = ((), (), s32[]{:S(2)}) async-start(), calls=%async_computation.10 | async-start | bytes 1179648 | tf_op jit(solution)/shard_map/reduce_scatter | solution.py:139
  150.1 169.8 %reduce-scatter.11.cloned.1.call-start = ((), (), s32[]{:S(2)}) async-start(), calls=%async_computation.8 | async-start | bytes 1179648 | tf_op jit(solution)/shard_map/reduce_scatter | solution.py:133
  151.6 218.7 %reduce-scatter.13.cloned.1.call-start = ((), (), s32[]{:S(2)}) async-start(), calls=%async_computation.9 | async-start | bytes 3538944 | tf_op jit(solution)/shard_map/reduce_scatter | solution.py:136
  154.8 1.5 copy-start.5
  169.4 41.4 %collective-permute-start.2 = (f32[128,2048]{1,0:T(8,128)}, f32[128,2048]{1,0:T(8,128)}, u32[]{:S(2)}, u32[]{:S(2)}) collective-permute-start(f32[128,2048]{1,0:T(8,128)} %copy.180), channel_id=1, source_target_pairs={{0,1},{1,0},{2,3},{3,2},{4,5},{5,4},{6,7},{7,6},{8,9},{9,8},{10,11... | collective-permute-start | bytes 3145736 | tf_op jit(solution)/shard_map/ppermute | solution.py:16
  169.4 72.3 %collective-permute-start.3 = (f32[128,2048]{1,0:T(8,128)}, f32[128,2048]{1,0:T(8,128)}, u32[]{:S(2)}, u32[]{:S(2)}) collective-permute-start(f32[128,2048]{1,0:T(8,128)} %copy.181), channel_id=1, source_target_pairs={{0,2},{2,0},{1,3},{3,1},{4,6},{6,4},{5,7},{7,5},{8,10},{10,8},{9,1... | collective-permute-start | bytes 3145736 | tf_op jit(solution)/shard_map/ppermute | solution.py:16
  182.2 74.2 %collective-permute-start.7 = (f32[128,2048]{1,0:T(8,128)}, f32[128,2048]{1,0:T(8,128)}, u32[]{:S(2)}, u32[]{:S(2)}) collective-permute-start(f32[128,2048]{1,0:T(8,128)} %copy.187), channel_id=1, source_target_pairs={{0,2},{2,0},{1,3},{3,1},{4,6},{6,4},{5,7},{7,5},{8,10},{10,8},{9,1... | collective-permute-start | bytes 3145736 | tf_op jit(solution)/shard_map/ppermute | solution.py:16
  182.7 73.6 %collective-permute-start.6 = (f32[128,2048]{1,0:T(8,128)}, f32[128,2048]{1,0:T(8,128)}, u32[]{:S(2)}, u32[]{:S(2)}) collective-permute-start(f32[128,2048]{1,0:T(8,128)} %copy.186), channel_id=1, source_target_pairs={{0,1},{1,0},{2,3},{3,2},{4,5},{5,4},{6,7},{7,6},{8,9},{9,8},{10,11... | collective-permute-start | bytes 3145736 | tf_op jit(solution)/shard_map/ppermute | solution.py:16
  192.0 64.3 %copy-start.8 = (f32[128,2048]{1,0:T(8,128)S(1)}, f32[128,2048]{1,0:T(8,128)}, u32[]{:S(2)}) copy-start(f32[128,2048]{1,0:T(8,128)} %copy.185) | copy-start | bytes 3145732
  192.0 64.3 %copy-start.11 = (bf16[2048,128]{1,0:T(8,128)(2,1)S(1)}, bf16[2048,128]{1,0:T(8,128)(2,1)}, u32[]{:S(2)}) copy-start(bf16[2048,128]{1,0:T(8,128)(2,1)} %param.11) | copy-start | bytes 1572868
Sparse Core Ops, SparseCore 0:
  119.5 44.6 reduce-scatter.6
  168.1 34.0 reduce-scatter.16
  205.9 34.0 reduce-scatter.8
  243.9 36.0 reduce-scatter.14
  283.9 35.9 reduce-scatter.10
  324.1 46.2 reduce-scatter.12
where the time goes:
time: 379 us; the launch traced here: 377 us
  waiting for transfers between devices  171 us (45%)
  blocking collectives  68 us (18%)
  matrix products  55.7 us (15%)
  local copies, waits for them, and re-layouts  40.7 us (11%)
  other arithmetic  15.9 us (4%)
  between operations  14.4 us (4%)
  starting transfers between devices  11.5 us (3%)
    ppermute x8, waiting for transfers between devices, partner(): return lax.ppermute(block, axis, route)  61.5 us
    reduce_scatter x1, waiting for transfers between devices, body(): lax.psum_scatter(down_block_terms.astype(jnp.bfloat16), 'dp', scatter_dim...  50.4 us
    psum x1, blocking collectives, body(): lax.psum((jnp.dot(tokens, up_left, preferred_element_type=jnp.float32), j...  49.9 us
    reduce_scatter x1, waiting for transfers between devices, body(): lax.psum_scatter(up_right_terms.astype(jnp.bfloat16), 'dp', scatter_dimen...  40 us
    dot_general x12, matrix products, blockwise(): jnp.einsum(form, pieces, blocks, preferred_element_type=jnp.float32)  28.2 us
    reshape x12, local copies, waits for them, and re-layouts, blockwise(): return result.reshape(row_count, block_count * width_out)  25.6 us
    reduce_scatter x1, waiting for transfers between devices, body(): lax.psum_scatter(down_left_terms.astype(jnp.bfloat16), 'dp', scatter_dime...  19.1 us
    psum x1, blocking collectives, body(): lax.psum(jnp.dot(hidden, down_left, preferred_element_type=jnp.float32),...  18.1 us
  transfers between devices with their start and end apart: 14, of which 6 were waited for; matrix products, arithmetic and copies ran while one was open for 22% of the time, Pallas kernels for 0%

commit v1 on v0

--- a/solution.py
+++ b/solution.py
@@ -1,8 +1,11 @@
+import functools
 import math
 
 import jax
 import jax.numpy as jnp
 from jax import lax
+from jax.experimental import pallas as pl
+from jax.experimental.pallas import tpu as pltpu
 from jax.sharding import PartitionSpec as P
 
 
@@ -147,6 +150,395 @@
     return (out, tokens_grad, grads[0], grads[1], grads[2], grads[3], grads[4], grads[5])
 
 
+MESH = pl.DeviceIdType.MESH
+BF = jnp.bfloat16
+F32 = jnp.float32
+
+
+def dot(left, right, left_dim, right_dim):
+    return lax.dot_general(
+        left, right, (((left_dim,), (right_dim,)), ((), ())), preferred_element_type=F32
+    )
+
+
+def fused_kernel(
+    grad_scale,
+    tok, cot, up, upl, upr, dn, dnl, dnr,
+    out, tgrad, upg, uplg, uprg, dng, dnlg, dnrg,
+    ptok, pcot, hp, hg, hid, pre, oacc, tacc, osend, orecv, tsend, trecv,
+    lowacc, lowsend, lowrecv, ldacc, ldsend, ldrecv, lpacc, lpsend, lprecv, lows,
+    g_d, g_u, g_s, a_d, a_u, a_s, b_d, b_u, b_s, c_d, c_u, c_s,
+    send_sem, recv_sem,
+):
+    blocks = up.shape[1]
+    side = up.shape[2]
+    wide = up.shape[3]
+    rank = upl.shape[1]
+    block_cols = 3 * blocks * wide
+    me = lax.axis_index("tensor")
+    dp = lax.axis_index("dp")
+    core = lax.rem(dp, 2)
+    x = lax.rem(lax.div(dp, 2), 2)
+    y = lax.div(dp, 4)
+    peers = [
+        me + 1 - 2 * lax.rem(me, 2),
+        me + 2 - 4 * lax.div(me, 2),
+        3 - me,
+    ]
+    core_n = dp + 1 - 2 * core
+    x_n = dp + 2 - 4 * x
+    y_n = dp + 4 - 8 * y
+    barrier = pltpu.get_barrier_semaphore()
+    for peer in peers:
+        pl.semaphore_signal(barrier, inc=1, device_id={"tensor": peer}, device_id_type=MESH)
+    for peer in (core_n, x_n, y_n):
+        pl.semaphore_signal(barrier, inc=1, device_id={"dp": peer}, device_id_type=MESH)
+    pl.semaphore_wait(barrier, 6)
+
+    count = [0]
+
+    def send(src, dst, axis, peer):
+        at = count[0]
+        count[0] += 1
+        copy = pltpu.make_async_remote_copy(
+            src_ref=src, dst_ref=dst, send_sem=send_sem.at[at], recv_sem=recv_sem.at[at],
+            device_id={axis: peer}, device_id_type=MESH,
+        )
+        copy.start()
+        return copy
+
+    def wait(copies):
+        for copy in copies:
+            copy.wait()
+
+    def cols(b, width):
+        return pl.ds(pl.multiple_of(b * width, width), width)
+
+    def loop(steps, step):
+        def run(i, carry):
+            step(i)
+            return carry
+        lax.fori_loop(0, steps, run, 0)
+
+    tok_copies = [send(tok, ptok.at[k], "tensor", peers[k]) for k in (1, 0)]
+    lowacc[:, :rank] = dot(tok[...], upl[...], 1, 0)
+    lowacc[:, rank:] = dot(cot[...], dnr[...], 1, 1)
+    lowsend[...] = lowacc[...].astype(BF)
+    low_copies = [send(lowsend, lowrecv.at[k], "tensor", peers[k]) for k in range(3)]
+    cot_copies = [send(cot, pcot.at[k], "tensor", peers[k]) for k in (1, 0)]
+
+    def own_factor(b):
+        hp[:, cols(b, wide)] = dot(tok[:, cols(b, side)], up[0, b], 1, 0)
+        hg[:, cols(b, wide)] = dot(cot[:, cols(b, side)], dn[0, b], 1, 1)
+
+    loop(blocks, own_factor)
+    wait(low_copies)
+    low_all = lowacc[...]
+    for k in range(3):
+        low_all = low_all + lowrecv[k].astype(F32)
+    lows[0] = low_all[:, :rank].astype(BF)
+    lows[1] = low_all[:, rank:].astype(BF)
+
+    def low_factor(b):
+        hp[:, cols(b, wide)] += dot(lows[0], upr[:, cols(b, wide)], 1, 0)
+        hg[:, cols(b, wide)] += dot(lows[1], dnl[cols(b, wide), :], 1, 1)
+
+    loop(blocks, low_factor)
+    ldacc[...] = jnp.zeros_like(ldacc)
+    lpacc[...] = jnp.zeros_like(lpacc)
+    wait(tok_copies)
+
+    def forward(b):
+        h = hp[:, cols(b, wide)]
+        h = h + dot(ptok[0, :, cols(b, side)], up[1, b], 1, 0)
+        h = h + dot(ptok[1, :, cols(b, side)], up[2, b], 1, 0)
+        share = 0.5 + 0.5 * lax.erf(h * math.sqrt(0.5))
+        hidden = (h * share).astype(BF)
+        hid[:, cols(b, wide)] = hidden
+        hp[:, cols(b, wide)] = share + h * (jnp.exp(-0.5 * h * h) * (1.0 / math.sqrt(2 * math.pi)))
+        ldacc[...] += dot(hidden, dnl[cols(b, wide), :], 1, 0)
+        osend[0, :, cols(b, side)] = dot(hidden, dn[1, b], 1, 0).astype(BF)
+        osend[1, :, cols(b, side)] = dot(hidden, dn[2, b], 1, 0).astype(BF)
+        oacc[:, cols(b, side)] = dot(hidden, dn[0, b], 1, 0)
+
+    loop(blocks, forward)
+    ldsend[...] = ldacc[...].astype(BF)
+    ld_copies = [send(ldsend, ldrecv.at[k], "tensor", peers[k]) for k in range(3)]
+    out_copies = [send(osend.at[k], orecv.at[k], "tensor", peers[k]) for k in (1, 0)]
+
+    def keep(buffer, at, term, part, parts):
+        rows = term.shape[0] // 8
+        for p in range(8):
+            first = p * rows + part * (rows // parts)
+            buffer[p % 2, p // 4, p // 2 % 2, :, at] = (
+                term[first : first + rows // parts] * grad_scale
+            ).astype(BF)
+
+    wait(cot_copies)
+
+    def down_terms(b):
+        hidden = hid[:, cols(b, wide)]
+        for k in range(3):
+            source = cot[:, cols(b, side)] if k == 0 else pcot[k - 1, :, cols(b, side)]
+            term = dot(hidden, source, 0, 0)
+            for part in range(2):
+                at = pl.ds(pl.multiple_of((k * blocks + b) * wide + part * side, side), side)
+                keep(g_d, at, term, part, 2)
+        at = pl.ds(pl.multiple_of(block_cols + b * wide, wide), wide)
+        keep(g_d, at, dot(lows[1], hidden, 0, 0), 0, 1)
+
+    loop(blocks, down_terms)
+
+    def start_core(group, arrived):
+        return [send(group.at[1 - core], arrived, "dp", core_n)]
+
+    def start_chip(group, arrived):
+        half = group.shape[4] // 2
+        copies = []
+        for other in range(2):
+            copies.append(
+                send(group.at[core, other, 1 - x, :, pl.ds(0, half)], arrived.at[other], "dp", x_n)
+            )
+            copies.append(
+                send(
+                    group.at[core, 1 - y, other, :, pl.ds(half, half)],
+                    arrived.at[2 + other], "dp", y_n,
+                )
+            )
+        return copies
+
+    def start_last(group, arrived):
+        half = group.shape[4] // 2
+        return [
+            send(group.at[core, 1 - y, x, :, pl.ds(0, half)], arrived.at[0], "dp", y_n),
+            send(group.at[core, y, 1 - x, :, pl.ds(half, half)], arrived.at[1], "dp", x_n),
+        ]
+
+    def add_core(group, arrived):
+        def step(i):
+            at = cols(i, 512)
+            for yy in range(2):
+                for xx in range(2):
+                    group[core, yy, xx, :, at] = (
+                        group[core, yy, xx, :, at].astype(F32) + arrived[yy, xx, :, at].astype(F32)
+                    ).astype(BF)
+        loop(group.shape[4] // 512, step)
+
+    def add_chip(group, arrived):
+        half = group.shape[4] // 2
+        def step(i):
+            at = cols(i, 512)
+            late = pl.ds(pl.multiple_of(half + i * 512, 512), 512)
+            for other in range(2):
+                group[core, other, x, :, at] = (
+                    group[core, other, x, :, at].astype(F32) + arrived[other, :, at].astype(F32)
+                ).astype(BF)
+                group[core, y, other, :, late] = (
+                    group[core, y, other, :, late].astype(F32)
+                    + arrived[2 + other, :, at].astype(F32)
+                ).astype(BF)
+        loop(half // 512, step)
+
+    def total(group, arrived, part, i):
+        half = group.shape[4] // 2
+        at = pl.ds(pl.multiple_of(part * half + i * wide, wide), wide)
+        return (
+            group[core, y, x, :, at].astype(F32) + arrived[part, :, cols(i, wide)].astype(F32)
+        ).astype(BF)
+
+    def finish(group, arrived, put_block, put_side):
+        per_half = group.shape[4] // 2 // wide
+        for part in range(2):
+            edge = min(max(3 * blocks - part * per_half, 0), per_half)
+            if edge:
+                loop(edge, lambda i: put_block(part * per_half + i, total(group, arrived, part, i)))
+            if edge < per_half:
+                def side_step(i):
+                    put_side(
+                        part * per_half + edge + i - 3 * blocks,
+                        total(group, arrived, part, edge + i),
+                    )
+                loop(per_half - edge, side_step)
+
+    a_d_copies = start_core(g_d, a_d)
+
+    def backward(b):
+        g = hg[:, cols(b, wide)]
+        g = g + dot(pcot[0, :, cols(b, side)], dn[1, b], 1, 1)
+        g = g + dot(pcot[1, :, cols(b, side)], dn[2, b], 1, 1)
+        grad = (g * hp[:, cols(b, wide)]).astype(BF)
+        pre[:, cols(b, wide)] = grad
+        lpacc[...] += dot(grad, upr[:, cols(b, wide)], 1, 1)
+        tsend[0, :, cols(b, side)] = dot(grad, up[1, b], 1, 1).astype(BF)
+        tsend[1, :, cols(b, side)] = dot(grad, up[2, b], 1, 1).astype(BF)
+        tacc[:, cols(b, side)] = dot(grad, up[0, b], 1, 1)
+
+    loop(blocks, backward)
+    lpsend[...] = lpacc[...].astype(BF)
+    lp_copies = [send(lpsend, lprecv.at[k], "tensor", peers[k]) for k in range(3)]
+    grad_copies = [send(tsend.at[k], trecv.at[k], "tensor", peers[k]) for k in (1, 0)]
+
+    wait(a_d_copies)
+    add_core(g_d, a_d)
+    b_d_copies = start_chip(g_d, b_d)
+
+    def up_terms(b):
+        grad = pre[:, cols(b, wide)]
+        for k in range(3):
+            source = tok[:, cols(b, side)] if k == 0 else ptok[k - 1, :, cols(b, side)]
+            at = pl.ds(pl.multiple_of((k * blocks + b) * wide, wide), wide)
+            keep(g_u, at, dot(source, grad, 0, 0), 0, 1)
+        at = pl.ds(pl.multiple_of(block_cols + b * wide, wide), wide)
+        keep(g_u, at, dot(lows[0], grad, 0, 0), 0, 1)
+
+    loop(blocks, up_terms)
+    a_u_copies = start_core(g_u, a_u)
+    wait(b_d_copies)
+    add_chip(g_d, b_d)
+    c_d_copies = start_last(g_d, c_d)
+    wait(a_u_copies)
+    add_core(g_u, a_u)
+    b_u_copies = start_chip(g_u, b_u)
+
+    def whole(acc, arrived):
+        value = acc[...]
+        for k in range(3):
+            value = value + arrived[k].astype(F32)
+        return value.astype(BF)
+
+    wait(ld_copies)
+    lows[2] = whole(ldacc, ldrecv)
+    wait(lp_copies)
+    lows[3] = whole(lpacc, lprecv)
+
+    def side_terms(b):
+        keep(g_s, cols(b, side), dot(lows[2], cot[:, cols(b, side)], 0, 0), 0, 1)
+        at = pl.ds(pl.multiple_of((blocks + b) * side, side), side)
+        keep(g_s, at, dot(lows[3], tok[:, cols(b, side)], 0, 0), 0, 1)
+
+    loop(blocks, side_terms)
+    a_s_copies = start_core(g_s, a_s)
+    wait(out_copies)
+
+    def put_out(b):
+        at = cols(b, side)
+        out[:, at] = (
+            oacc[:, at] + dot(lows[2], dnr[:, at], 1, 0)
+            + orecv[0, :, at].astype(F32) + orecv[1, :, at].astype(F32)
+        ).astype(BF)
+
+    loop(blocks, put_out)
+    wait(a_s_copies)
+    add_core(g_s, a_s)
+    b_s_copies = start_chip(g_s, b_s)
+    wait(c_d_copies)
+
+    def put_down(i, value):
+        dng[i, :16, :] = value[:, :side]
+        dng[i, 16:, :] = value[:, side:]
+
+    def put_down_left(i, value):
+        dnlg[:, cols(i, wide)] = value
+
+    finish(g_d, c_d, put_down, put_down_left)
+    wait(b_u_copies)
+    add_chip(g_u, b_u)
+    c_u_copies = start_last(g_u, c_u)
+    wait(b_s_copies)
+    add_chip(g_s, b_s)
+    c_s_copies = start_last(g_s, c_s)
+    wait(grad_copies)
+
+    def put_tokens(b):
+        at = cols(b, side)
+        rows = pl.ds(pl.multiple_of(b * side, side), side)
+        tgrad[:, at] = (
+            tacc[:, at] + dot(lows[3], upl[rows, :], 1, 1)
+            + trecv[0, :, at].astype(F32) + trecv[1, :, at].astype(F32)
+        ).astype(BF)
+
+    loop(blocks, put_tokens)
+    wait(c_u_copies)
+
+    def put_up(i, value):
+        upg[i] = value
+
+    def put_up_right(i, value):
+        uprg[:, cols(i, wide)] = value
+
+    finish(g_u, c_u, put_up, put_up_right)
+    wait(c_s_copies)
+
+    def put_sides(i):
+        dnrg[:, cols(i, wide)] = total(g_s, c_s, 0, i)
+        uplg[:, cols(i, wide)] = total(g_s, c_s, 1, i)
+
+    loop(blocks * side // wide, put_sides)
+
+
+def fused(tokens, cotangent, up_blocks, up_left, up_right, down_blocks, down_left, down_right):
+    rows, width = tokens.shape
+    factors, blocks, side, wide = up_blocks.shape
+    rank = up_left.shape[1]
+    hidden = blocks * wide
+    n_dp = lax.axis_size("dp")
+    grad_scale = 1.0 / math.sqrt(rows * n_dp)
+    share = rank // n_dp
+    group_cols = (factors * hidden + hidden, factors * hidden + hidden, 2 * width)
+    vmem = pltpu.VMEM
+    scratch = [
+        vmem((2, rows, width), BF), vmem((2, rows, width), BF),
+        vmem((rows, hidden), F32), vmem((rows, hidden), F32),
+        vmem((rows, hidden), BF), vmem((rows, hidden), BF),
+        vmem((rows, width), F32), vmem((rows, width), F32),
+        vmem((2, rows, width), BF), vmem((2, rows, width), BF),
+        vmem((2, rows, width), BF), vmem((2, rows, width), BF),
+        vmem((rows, 2 * rank), F32), vmem((rows, 2 * rank), BF), vmem((3, rows, 2 * rank), BF),
+        vmem((rows, rank), F32), vmem((rows, rank), BF), vmem((3, rows, rank), BF),
+        vmem((rows, rank), F32), vmem((rows, rank), BF), vmem((3, rows, rank), BF),
+        vmem((4, rows, rank), BF),
+    ]
+    scratch += [vmem((2, 2, 2, share, c), BF) for c in group_cols]
+    scratch += [vmem((2, 2, share, c), BF) for c in group_cols]
+    scratch += [vmem((4, share, c // 2), BF) for c in group_cols]
+    scratch += [vmem((2, share, c // 2), BF) for c in group_cols]
+    scratch += [pltpu.SemaphoreType.DMA((38,)), pltpu.SemaphoreType.DMA((38,))]
+    shapes = [
+        (rows, width), (rows, width), (factors * blocks, side // n_dp, wide), (share, width),
+        (share, hidden), (factors * blocks, wide // n_dp, side), (share, hidden), (share, width),
+    ]
+    got = pl.pallas_call(
+        functools.partial(fused_kernel, grad_scale),
+        out_shape=[jax.ShapeDtypeStruct(shape, BF) for shape in shapes],
+        in_specs=[pl.BlockSpec(memory_space=pltpu.VMEM)] * 8,
+        out_specs=[pl.BlockSpec(memory_space=pltpu.VMEM)] * 8,
+        scratch_shapes=scratch,
+        compiler_params=pltpu.CompilerParams(
+            collective_id=0, has_side_effects=True, vmem_limit_bytes=60 * 1024 * 1024
+        ),
+    )(tokens, cotangent, up_blocks, up_left, up_right, down_blocks, down_left, down_right)
+    return (
+        got[0],
+        got[1],
+        got[2].reshape(factors, blocks, side // n_dp, wide),
+        got[3].T,
+        got[4],
+        got[5].reshape(factors, blocks, wide // n_dp, side),
+        got[6].T,
+        got[7],
+    )
+
+
+def fits(mesh, tokens, up_blocks, up_left):
+    return (
+        mesh.shape["dp"] == 8
+        and mesh.shape["tensor"] == 4
+        and tokens.shape[0] == 8 * 128
+        and up_blocks.shape == (3, 64, 128, 256)
+        and up_left.shape[1] == 128
+    )
+
+
 def solution(mesh):
     in_specs = (
         P("dp", "tensor"),
@@ -168,4 +560,11 @@
         P("tensor", "dp"),
         P("dp", "tensor"),
     )
-    return jax.shard_map(body, mesh=mesh, in_specs=in_specs, out_specs=out_specs, check_vma=False)
+
+    def run(*arrays):
+        local = fused if fits(mesh, arrays[0], arrays[2], arrays[3]) else body
+        return jax.shard_map(
+            local, mesh=mesh, in_specs=in_specs, out_specs=out_specs, check_vma=False
+        )(*arrays)
+
+    return run

time: 379 us -> 137 us (0.36)
  waiting for transfers between devices: 171 us -> 0 us
  Pallas kernels: 0 us -> 125 us
  blocking collectives: 68 us -> 0 us
  matrix products: 55.7 us -> 0 us
  local copies, waits for them, and re-layouts: 40.7 us -> 10.7 us
  other arithmetic: 15.9 us -> 0 us
  between operations: 14.4 us -> 0.67 us
  starting transfers between devices: 11.5 us -> 0 us
    pallas_call x0 -> x1, Pallas kernels: none -> 125 us  [fused(): pl.pallas_call(functools.partial(fused_kernel, grad_scale), out_shape=[ja...]
    reduce_scatter x6 -> x0, waiting for transfers between devices: 109 us -> none  [the longest x1 50.4 us: body(): lax.psum_scatter(down_block_terms.astype(jnp.bfloat16), 'dp', scatter_dim...]
    psum x2 -> x0, blocking collectives: 68 us -> none  [the longest x1 49.9 us: body(): lax.psum((jnp.dot(tokens, up_left, preferred_element_type=jnp.float32), j...]
    ppermute x8 -> x0, waiting for transfers between devices: 61.5 us -> none  [partner(): return lax.ppermute(block, axis, route)]
    dot_general x30 -> x0, matrix products: 55.7 us -> none  [the longest x12 28.2 us: blockwise(): jnp.einsum(form, pieces, blocks, preferred_element_type=jnp.float32)]
    reshape x14 -> x0, local copies, waits for them, and re-layouts: 27.8 us -> none  [the longest x12 25.6 us: blockwise(): return result.reshape(row_count, block_count * width_out)]
    convert_element_type x4 -> x0, other arithmetic: 15.9 us -> none  [the longest x1 9.26 us: body(): pre_grad = gelu_back(hidden_grad)[0].astype(jnp.bfloat16)]
    ppermute x8 -> x0, starting transfers between devices: 11 us -> none  [partner(): return lax.ppermute(block, axis, route)]
  transfers between devices with their start and end apart: 14 -> 0, of which waited for: 6 -> 0; matrix products, arithmetic and copies ran while one was open for 22% -> 0% of each run, Pallas kernels for 0% -> 0%
where the time goes in v1:
time: 137 us
  Pallas kernels  125 us (91%)
  local copies, waits for them, and re-layouts  10.7 us (8%)
    pallas_call x1, Pallas kernels, fused(): pl.pallas_call(functools.partial(fused_kernel, grad_scale), out_shape=[ja...  125 us
    unnamed x14, local copies, waits for them, and re-layouts  10.7 us

profile of v1, /device:TPU:0, one launch (start us, length us, event | category | flops | bytes accessed | tf_op | source)
XLA Modules:
  0.0 136.5 jit_solution(7609584405955848024)
XLA Ops:
  0.6 125.2 %shard_map.143 = (bf16[128,2048]{1,0:T(8,128)(2,1)}, bf16[128,2048]{1,0:T(8,128)(2,1)}, bf16[48,16,256]{2,1,0:T(8,128)(2,1)}, bf16[16,2048]{1,0:T(8,128)(2,1)}, ...) custom-call(bf16[128,2048]{1,0:T(8,128)(2,1)} %tok.1, ...), custom_call_target="tpu_custom_call" | custom-call | tf_op jit(solution)/shard_map/pallas_call | solution.py:510
  125.8 0.0 copy-start
  125.9 0.0 copy-start.1
  125.9 0.0 copy-start.2
  125.9 1.9 %copy.24 = bf16[128,2048]{1,0:T(8,128)(2,1)} copy(bf16[128,2048]{1,0:T(8,128)(2,1)} %get-tuple-element.32) | data formatting | bytes 1048576
  127.8 1.9 %copy.25 = bf16[128,2048]{1,0:T(8,128)(2,1)} copy(bf16[128,2048]{1,0:T(8,128)(2,1)} %get-tuple-element.33) | data formatting | bytes 1048576
  129.7 1.8 %copy.26 = bf16[3,16,16,256]{3,2,1,0:T(8,128)(2,1)} copy(bf16[3,16,16,256]{3,2,1,0:T(8,128)(2,1)} %bitcast.5) | data formatting | bytes 786432
  131.5 1.5 %copy.27 = bf16[2048,16]{0,1:T(8,128)(2,1)} copy(bf16[2048,16]{0,1:T(8,128)(2,1)} %bitcast.7) | data formatting | bytes 131072
  132.9 1.6 %copy.28 = bf16[16,4096]{1,0:T(8,128)(2,1)} copy(bf16[16,4096]{1,0:T(8,128)(2,1)} %get-tuple-element.36) | data formatting | bytes 262144
  134.5 0.0 copy-done
  134.5 0.7 copy.29
  135.3 0.0 copy-done.1
  135.3 0.7 copy.30
  135.9 0.0 copy-done.2
  135.9 0.6 copy.31
Async XLA Ops:
  125.8 8.7 %copy-start = (bf16[48,32,128]{2,1,0:T(8,128)(2,1)S(1)}, bf16[48,32,128]{2,1,0:T(8,128)(2,1)}, u32[]{:S(2)}) copy-start(bf16[48,32,128]{2,1,0:T(8,128)(2,1)} %get-tuple-element.21) | copy-start | bytes 1179652
  125.9 9.4 %copy-start.1 = (bf16[16,4096]{1,0:T(8,128)(2,1)S(1)}, bf16[16,4096]{1,0:T(8,128)(2,1)}, u32[]{:S(2)}) copy-start(bf16[16,4096]{1,0:T(8,128)(2,1)} %get-tuple-element.22) | copy-start | bytes 393220
  125.9 10.0 %copy-start.2 = (bf16[16,2048]{1,0:T(8,128)(2,1)S(1)}, bf16[16,2048]{1,0:T(8,128)(2,1)}, u32[]{:S(2)}) copy-start(bf16[16,2048]{1,0:T(8,128)(2,1)} %get-tuple-element.39) | copy-start | bytes 196612

commit v2 on v1

--- a/solution.py
+++ b/solution.py
@@ -163,12 +163,13 @@
 
 def fused_kernel(
     grad_scale,
-    tok, cot, up, upl, upr, dn, dnl, dnr,
+    tok, cot, up_far, upl, upr_far, dn_far, dnl_far, dnr,
     out, tgrad, upg, uplg, uprg, dng, dnlg, dnrg,
     ptok, pcot, hp, hg, hid, pre, oacc, tacc, osend, orecv, tsend, trecv,
     lowacc, lowsend, lowrecv, ldacc, ldsend, ldrecv, lpacc, lpsend, lprecv, lows,
-    g_d, g_u, g_s, a_d, a_u, a_s, b_d, b_u, b_s, c_d, c_u, c_s,
-    send_sem, recv_sem,
+    up, upr, dn, dnl,
+    g_d, g_e, g_u, g_s, a_d, a_e, a_u, a_s, b_d, b_e, b_u, b_s, c_d, c_e, c_u, c_s,
+    send_sem, recv_sem, load_sem,
 ):
     blocks = up.shape[1]
     side = up.shape[2]
@@ -188,6 +189,14 @@
     core_n = dp + 1 - 2 * core
     x_n = dp + 2 - 4 * x
     y_n = dp + 4 - 8 * y
+    loads = [
+        pltpu.make_async_copy(far, near, load_sem.at[at])
+        for at, (far, near) in enumerate(
+            ((up_far, up), (dn_far, dn), (upr_far, upr), (dnl_far, dnl))
+        )
+    ]
+    for load in loads:
+        load.start()
     barrier = pltpu.get_barrier_semaphore()
     for peer in peers:
         pl.semaphore_signal(barrier, inc=1, device_id={"tensor": peer}, device_id_type=MESH)
@@ -231,6 +240,7 @@
         hp[:, cols(b, wide)] = dot(tok[:, cols(b, side)], up[0, b], 1, 0)
         hg[:, cols(b, wide)] = dot(cot[:, cols(b, side)], dn[0, b], 1, 1)
 
+    wait(loads)
     loop(blocks, own_factor)
     wait(low_copies)
     low_all = lowacc[...]
@@ -264,7 +274,6 @@
     loop(blocks, forward)
     ldsend[...] = ldacc[...].astype(BF)
     ld_copies = [send(ldsend, ldrecv.at[k], "tensor", peers[k]) for k in range(3)]
-    out_copies = [send(osend.at[k], orecv.at[k], "tensor", peers[k]) for k in (1, 0)]
 
     def keep(buffer, at, term, part, parts):
         rows = term.shape[0] // 8
@@ -274,18 +283,20 @@
                 term[first : first + rows // parts] * grad_scale
             ).astype(BF)
 
-    wait(cot_copies)
+    def keep_down(buffer, b, k, source):
+        term = dot(hid[:, cols(b, wide)], source, 0, 0)
+        for part in range(2):
+            at = pl.ds(pl.multiple_of((k * blocks + b) * wide + part * side, side), side)
+            keep(buffer, at, term, part, 2)
 
     def down_terms(b):
-        hidden = hid[:, cols(b, wide)]
-        for k in range(3):
-            source = cot[:, cols(b, side)] if k == 0 else pcot[k - 1, :, cols(b, side)]
-            term = dot(hidden, source, 0, 0)
-            for part in range(2):
-                at = pl.ds(pl.multiple_of((k * blocks + b) * wide + part * side, side), side)
-                keep(g_d, at, term, part, 2)
-        at = pl.ds(pl.multiple_of(block_cols + b * wide, wide), wide)
-        keep(g_d, at, dot(lows[1], hidden, 0, 0), 0, 1)
+        keep_down(g_d, b, 0, cot[:, cols(b, side)])
+        at = pl.ds(pl.multiple_of((blocks + b) * wide, wide), wide)
+        keep(g_d, at, dot(lows[1], hid[:, cols(b, wide)], 0, 0), 0, 1)
+
+    def partner_down_terms(b):
+        for k in range(2):
+            keep_down(g_e, b, k, pcot[k, :, cols(b, side)])
 
     loop(blocks, down_terms)
 
@@ -346,21 +357,31 @@
             group[core, y, x, :, at].astype(F32) + arrived[part, :, cols(i, wide)].astype(F32)
         ).astype(BF)
 
-    def finish(group, arrived, put_block, put_side):
+    def finish(group, arrived, count, put_block, put_side):
         per_half = group.shape[4] // 2 // wide
         for part in range(2):
-            edge = min(max(3 * blocks - part * per_half, 0), per_half)
+            edge = min(max(count - part * per_half, 0), per_half)
             if edge:
                 loop(edge, lambda i: put_block(part * per_half + i, total(group, arrived, part, i)))
             if edge < per_half:
                 def side_step(i):
                     put_side(
-                        part * per_half + edge + i - 3 * blocks,
+                        part * per_half + edge + i - count,
                         total(group, arrived, part, edge + i),
                     )
                 loop(per_half - edge, side_step)
 
     a_d_copies = start_core(g_d, a_d)
+    wait(a_d_copies)
+    add_core(g_d, a_d)
+    b_d_copies = start_chip(g_d, b_d)
+    wait(cot_copies)
+    out_copies = [send(osend.at[k], orecv.at[k], "tensor", peers[k]) for k in (1, 0)]
+    loop(blocks, partner_down_terms)
+    a_e_copies = start_core(g_e, a_e)
+    wait(b_d_copies)
+    add_chip(g_d, b_d)
+    c_d_copies = start_last(g_d, c_d)
 
     def backward(b):
         g = hg[:, cols(b, wide)]
@@ -378,9 +399,9 @@
     lp_copies = [send(lpsend, lprecv.at[k], "tensor", peers[k]) for k in range(3)]
     grad_copies = [send(tsend.at[k], trecv.at[k], "tensor", peers[k]) for k in (1, 0)]
 
-    wait(a_d_copies)
-    add_core(g_d, a_d)
-    b_d_copies = start_chip(g_d, b_d)
+    wait(a_e_copies)
+    add_core(g_e, a_e)
+    b_e_copies = start_chip(g_e, b_e)
 
     def up_terms(b):
         grad = pre[:, cols(b, wide)]
@@ -393,9 +414,9 @@
 
     loop(blocks, up_terms)
     a_u_copies = start_core(g_u, a_u)
-    wait(b_d_copies)
-    add_chip(g_d, b_d)
-    c_d_copies = start_last(g_d, c_d)
+    wait(b_e_copies)
+    add_chip(g_e, b_e)
+    c_e_copies = start_last(g_e, c_e)
     wait(a_u_copies)
     add_core(g_u, a_u)
     b_u_copies = start_chip(g_u, b_u)
@@ -418,6 +439,30 @@
 
     loop(blocks, side_terms)
     a_s_copies = start_core(g_s, a_s)
+    wait(c_d_copies)
+
+    def put_down(i, value):
+        dng[i, :16, :] = value[:, :side]
+        dng[i, 16:, :] = value[:, side:]
+
+    def put_partner_down(i, value):
+        put_down(blocks + i, value)
+
+    def put_down_left(i, value):
+        dnlg[:, cols(i, wide)] = value
+
+    finish(g_d, c_d, blocks, put_down, put_down_left)
+    wait(a_s_copies)
+    add_core(g_s, a_s)
+    b_s_copies = start_chip(g_s, b_s)
+    wait(c_e_copies)
+    finish(g_e, c_e, 2 * blocks, put_partner_down, put_down_left)
+    wait(b_u_copies)
+    add_chip(g_u, b_u)
+    c_u_copies = start_last(g_u, c_u)
+    wait(b_s_copies)
+    add_chip(g_s, b_s)
+    c_s_copies = start_last(g_s, c_s)
     wait(out_copies)
 
     def put_out(b):
@@ -428,25 +473,15 @@
         ).astype(BF)
 
     loop(blocks, put_out)
-    wait(a_s_copies)
-    add_core(g_s, a_s)
-    b_s_copies = start_chip(g_s, b_s)
-    wait(c_d_copies)
-
-    def put_down(i, value):
-        dng[i, :16, :] = value[:, :side]
-        dng[i, 16:, :] = value[:, side:]
-
-    def put_down_left(i, value):
-        dnlg[:, cols(i, wide)] = value
-
-    finish(g_d, c_d, put_down, put_down_left)
-    wait(b_u_copies)
-    add_chip(g_u, b_u)
-    c_u_copies = start_last(g_u, c_u)
-    wait(b_s_copies)
-    add_chip(g_s, b_s)
-    c_s_copies = start_last(g_s, c_s)
+    wait(c_u_copies)
+
+    def put_up(i, value):
+        upg[i] = value
+
+    def put_up_right(i, value):
+        uprg[:, cols(i, wide)] = value
+
+    finish(g_u, c_u, 3 * blocks, put_up, put_up_right)
     wait(grad_copies)
 
     def put_tokens(b):
@@ -458,15 +493,6 @@
         ).astype(BF)
 
     loop(blocks, put_tokens)
-    wait(c_u_copies)
-
-    def put_up(i, value):
-        upg[i] = value
-
-    def put_up_right(i, value):
-        uprg[:, cols(i, wide)] = value
-
-    finish(g_u, c_u, put_up, put_up_right)
     wait(c_s_copies)
 
     def put_sides(i):
@@ -484,7 +510,7 @@
     n_dp = lax.axis_size("dp")
     grad_scale = 1.0 / math.sqrt(rows * n_dp)
     share = rank // n_dp
-    group_cols = (factors * hidden + hidden, factors * hidden + hidden, 2 * width)
+    group_cols = (2 * hidden, (factors - 1) * hidden, (factors + 1) * hidden, 2 * width)
     vmem = pltpu.VMEM
     scratch = [
         vmem((2, rows, width), BF), vmem((2, rows, width), BF),
@@ -497,12 +523,14 @@
         vmem((rows, rank), F32), vmem((rows, rank), BF), vmem((3, rows, rank), BF),
         vmem((rows, rank), F32), vmem((rows, rank), BF), vmem((3, rows, rank), BF),
         vmem((4, rows, rank), BF),
+        vmem(up_blocks.shape, BF), vmem(up_right.shape, BF),
+        vmem(down_blocks.shape, BF), vmem(down_left.shape, BF),
     ]
     scratch += [vmem((2, 2, 2, share, c), BF) for c in group_cols]
     scratch += [vmem((2, 2, share, c), BF) for c in group_cols]
     scratch += [vmem((4, share, c // 2), BF) for c in group_cols]
     scratch += [vmem((2, share, c // 2), BF) for c in group_cols]
-    scratch += [pltpu.SemaphoreType.DMA((38,)), pltpu.SemaphoreType.DMA((38,))]
+    scratch += [pltpu.SemaphoreType.DMA((count,)) for count in (45, 45, 4)]
     shapes = [
         (rows, width), (rows, width), (factors * blocks, side // n_dp, wide), (share, width),
         (share, hidden), (factors * blocks, wide // n_dp, side), (share, hidden), (share, width),
@@ -510,7 +538,10 @@
     got = pl.pallas_call(
         functools.partial(fused_kernel, grad_scale),
         out_shape=[jax.ShapeDtypeStruct(shape, BF) for shape in shapes],
-        in_specs=[pl.BlockSpec(memory_space=pltpu.VMEM)] * 8,
+        in_specs=[
+            pl.BlockSpec(memory_space=pl.ANY if at in (2, 4, 5, 6) else pltpu.VMEM)
+            for at in range(8)
+        ],
         out_specs=[pl.BlockSpec(memory_space=pltpu.VMEM)] * 8,
         scratch_shapes=scratch,
         compiler_params=pltpu.CompilerParams(

time: 137 us -> 133 us (0.971)
  the two profiles are of different devices: /device:TPU:0 before, /device:TPU:8 now
where the time goes in v2:
time: 133 us
  Pallas kernels  121 us (91%)
  local copies, waits for them, and re-layouts  10.7 us (8%)
    pallas_call x1, Pallas kernels, fused(): pl.pallas_call(functools.partial(fused_kernel, grad_scale), out_shape=[ja...  121 us
    unnamed x14, local copies, waits for them, and re-layouts  10.7 us

profile of v2, /device:TPU:8, one launch (start us, length us, event | category | flops | bytes accessed | tf_op | source)
XLA Modules:
  0.0 132.8 jit_solution(12987657698547463000)
XLA Ops:
  0.6 121.5 %shard_map.143 = (bf16[128,2048]{1,0:T(8,128)(2,1)}, bf16[128,2048]{1,0:T(8,128)(2,1)}, bf16[48,16,256]{2,1,0:T(8,128)(2,1)}, bf16[16,2048]{1,0:T(8,128)(2,1)}, ...) custom-call(bf16[128,2048]{1,0:T(8,128)(2,1)} %tok.1, ...), custom_call_target="tpu_custom_call" | custom-call | tf_op jit(solution)/shard_map/pallas_call | solution.py:538
  122.1 0.0 copy-start
  122.1 0.0 copy-start.1
  122.1 0.0 copy-start.2
  122.2 1.9 %copy.24 = bf16[128,2048]{1,0:T(8,128)(2,1)} copy(bf16[128,2048]{1,0:T(8,128)(2,1)} %get-tuple-element.32) | data formatting | bytes 1048576
  124.1 1.9 %copy.25 = bf16[128,2048]{1,0:T(8,128)(2,1)} copy(bf16[128,2048]{1,0:T(8,128)(2,1)} %get-tuple-element.33) | data formatting | bytes 1048576
  126.0 1.8 %copy.26 = bf16[3,16,16,256]{3,2,1,0:T(8,128)(2,1)} copy(bf16[3,16,16,256]{3,2,1,0:T(8,128)(2,1)} %bitcast.5) | data formatting | bytes 786432
  127.7 1.5 %copy.27 = bf16[2048,16]{0,1:T(8,128)(2,1)} copy(bf16[2048,16]{0,1:T(8,128)(2,1)} %bitcast.7) | data formatting | bytes 131072
  129.2 1.6 %copy.28 = bf16[16,4096]{1,0:T(8,128)(2,1)} copy(bf16[16,4096]{1,0:T(8,128)(2,1)} %get-tuple-element.36) | data formatting | bytes 262144
  130.8 0.0 copy-done
  130.8 0.7 copy.29
  131.5 0.0 copy-done.1
  131.5 0.7 copy.30
  132.2 0.0 copy-done.2
  132.2 0.6 copy.31
Async XLA Ops:
  122.1 8.7 %copy-start = (bf16[48,32,128]{2,1,0:T(8,128)(2,1)S(1)}, bf16[48,32,128]{2,1,0:T(8,128)(2,1)}, u32[]{:S(2)}) copy-start(bf16[48,32,128]{2,1,0:T(8,128)(2,1)} %get-tuple-element.21) | copy-start | bytes 1179652
  122.1 9.4 %copy-start.1 = (bf16[16,4096]{1,0:T(8,128)(2,1)S(1)}, bf16[16,4096]{1,0:T(8,128)(2,1)}, u32[]{:S(2)}) copy-start(bf16[16,4096]{1,0:T(8,128)(2,1)} %get-tuple-element.22) | copy-start | bytes 393220
  122.1 10.0 %copy-start.2 = (bf16[16,2048]{1,0:T(8,128)(2,1)S(1)}, bf16[16,2048]{1,0:T(8,128)(2,1)}, u32[]{:S(2)}) copy-start(bf16[16,2048]{1,0:T(8,128)(2,1)} %get-tuple-element.39) | copy-start | bytes 196612
